TPU v7x, 512 devices: a whole 4x8x8 slice. The times are simulated.
512 devices in a mesh: rep: 8 (over y_lo, core), shard: 64 (over y_hi, z, x).
Axes of the slice: x: 4, y: 8 (y_hi: 2, y_lo: 4; y = y_hi * 4 + y_lo), z: 8, core: 2. Of those that a mesh axis runs over, the one named last changes fastest.
Arguments:
- grad_parts: bfloat16 [8, 64, 576, 1152], P('rep', 'shard'), may hold values from -64 to 64
- master: float32 [576, 1152], P('shard'), may hold values from -0.06 to 0.06
- moment_one: float32 [576, 1152], P('shard'), may hold values from -0.12 to 0.12
- moment_two: float32 [576, 1152], P('shard'), may hold values from 0.0001 to 0.01
- step_count: int32 [1], replicated, may hold values from 1 to 20
Outputs:
- new_master: float32 [576, 1152], P('shard')
- new_moment_one: float32 [576, 1152], P('shard')
- new_moment_two: float32 [576, 1152], P('shard')
- adam_direction: float32 [576, 1152], P('shard')
- params: bfloat16 [576, 1152], replicated
All inputs are finite; a program needn't handle non-finite values.
Results may differ from a plain program's by a relative error of at most 0.024.
Values may be sent and summed in bfloat16 or wider, within the bound.
A program may use at most 64 MiB of HBM per device.

v0:
```python
import jax
import jax.numpy as jnp
from jax import lax
from jax.sharding import PartitionSpec as P

BETA_ONE = 0.9
BETA_TWO = 0.95
LEARN_RATE = 0.001
EPSILON = 1e-08


def adam_step(gradient, master, moment_one, moment_two, step_count):
    new_moment_one = BETA_ONE * moment_one + (1.0 - BETA_ONE) * gradient
    new_moment_two = BETA_TWO * moment_two + (1.0 - BETA_TWO) * gradient * gradient
    steps_float = step_count[0].astype(jnp.float32)
    first_fix = 1.0 - jnp.power(jnp.float32(BETA_ONE), steps_float)
    second_fix = 1.0 - jnp.power(jnp.float32(BETA_TWO), steps_float)
    direction = new_moment_one / first_fix / (jnp.sqrt(new_moment_two / second_fix) + EPSILON)
    new_master = master - LEARN_RATE * direction
    return (new_master, new_moment_one, new_moment_two, direction)


def local(grad_parts, master, moment_one, moment_two, step_count):
    partial_value = grad_parts.reshape(grad_parts.shape[2], grad_parts.shape[3]).astype(jnp.float32)
    devices_total = lax.axis_size("rep") * lax.axis_size("shard")
    row_block = lax.psum_scatter(partial_value, "shard", scatter_dimension=0, tiled=True)
    summed = lax.psum(row_block, "rep")
    results = adam_step(summed / devices_total, master, moment_one, moment_two, step_count)
    new_master, new_moment_one, new_moment_two, direction = results
    params = lax.all_gather(new_master.astype(jnp.bfloat16), "shard", axis=0, tiled=True)
    return (new_master, new_moment_one, new_moment_two, direction, params)


def solution(mesh):
    placed = (
        P("rep", "shard", None, None),
        P("shard", None),
        P("shard", None),
        P("shard", None),
        P(),
    )
    return jax.shard_map(
        local,
        mesh=mesh,
        in_specs=placed,
        out_specs=(P("shard", None), P("shard", None), P("shard", None), P("shard", None), P()),
        check_vma=False,
    )
```

profile of v0, /device:TPU:8, one launch (start us, length us, event | category | flops | bytes accessed | tf_op | source)
XLA Modules:
  0.0 1022.8 jit_solution(6413098635314897203)
XLA Ops:
  7.2 0.0 copy-start
  7.2 0.0 copy-start.2
  7.2 0.0 copy-start.1
  7.2 0.0 all-reduce.3.cloned.1.call-start
  7.2 3.1 bitcast_convert_fusion
  10.3 0.0 all-reduce.3.cloned.1.call-update
  10.3 0.0 all-gather.3.cloned.1.call-start
  11.1 1.3 dynamic-slice
  13.0 837.0 %all-reduce.3.cloned.1.call-done = f32[576,1152]{1,0:T(8,128)} async-done(((f32[576,1152]{1,0:T(8,128)}), f32[576,1152]{1,0:T(8,128)}) %all-reduce.3.cloned.1.call-update) | async-done | bytes 2654224
  850.1 0.9 constant_dynamic-slice_fusion
  851.0 23.2 %psum.7 = f32[9,1152]{1,0:T(8,128)S(1)} all-reduce(f32[9,1152]{1,0:T(8,128)S(1)} %constant_dynamic-slice_fusion), channel_id=1, replica_groups=mesh['rep'=8,'shard'=64] {'rep'}, use_global_device_ids=true, to_apply=%region_1.0 | all-reduce | flops 10368 | bytes 82944 | tf_op jit(solution)/shard_map/psum | solution.py:27
  874.2 0.0 copy-done
  874.2 0.0 copy-done.2
  874.2 0.0 copy-done.1
  874.2 0.7 convert_bitcast_fusion
  874.9 0.0 all-gather.3.cloned.1.call-update
  875.0 137.3 %all-gather.3.cloned.1.call-done = bf16[64,9,1152]{2,1,0:T(8,128)(2,1)} async-done(((bf16[1,9,1152]{2,1,0:T(8,128)(2,1)}), bf16[64,9,1152]{2,1,0:T(8,128)(2,1)}) %all-gather.3.cloned.1.call-update) | async-done | bytes 1327120 | tf_op jit(solution)/shard_map/all_gather | solution.py:30
  1012.2 3.7 reshape.24
Async XLA Ops:
  7.2 867.0 %copy-start = (f32[9,1152]{1,0:T(8,128)S(1)}, f32[9,1152]{1,0:T(8,128)}, u32[]{:S(2)}) copy-start(f32[9,1152]{1,0:T(8,128)} %param.6) | copy-start | bytes 124420
  7.2 867.0 %copy-start.2 = (f32[9,1152]{1,0:T(8,128)S(1)}, f32[9,1152]{1,0:T(8,128)}, u32[]{:S(2)}) copy-start(f32[9,1152]{1,0:T(8,128)} %param.7) | copy-start | bytes 124420
  7.2 867.0 %copy-start.1 = (f32[9,1152]{1,0:T(8,128)S(1)}, f32[9,1152]{1,0:T(8,128)}, u32[]{:S(2)}) copy-start(f32[9,1152]{1,0:T(8,128)} %param.8) | copy-start | bytes 124420
  7.2 842.9 %all-reduce.3.cloned.1.call-start = ((), (), s32[]{:S(2)}) async-start(), calls=%async_computation.1 | async-start | bytes 5308416
  10.3 1001.9 %all-gather.3.cloned.1.call-start = ((), (), s32[]{:S(2)}) async-start(), calls=%async_computation | async-start | bytes 2396160 | tf_op jit(solution)/shard_map/all_gather | solution.py:30
Sparse Core Ops, SparseCore 0:
  11.0 839.0 all-reduce.2
  875.1 137.1 all-gather.2
where the time goes:
time: 1020 us
  waiting for transfers between devices  974 us (95%)
  blocking collectives  23.2 us (2%)
  between operations  15.5 us (2%)
    unnamed x3, waiting for transfers between devices  837 us
    all_gather x1, waiting for transfers between devices, local(): lax.all_gather(new_master.astype(jnp.bfloat16), 'shard', axis=0, tiled=True)  137 us
    psum x1, blocking collectives, local(): summed = lax.psum(row_block, 'rep')  23.2 us
  transfers between devices with their start and end apart: 2, of which 2 were waited for; matrix products, arithmetic and copies ran while one was open for 0% of the time, Pallas kernels for 0%

commit v1 on v0

--- a/solution.py
+++ b/solution.py
@@ -27,7 +27,12 @@
     summed = lax.psum(row_block, "rep")
     results = adam_step(summed / devices_total, master, moment_one, moment_two, step_count)
     new_master, new_moment_one, new_moment_two, direction = results
-    params = lax.all_gather(new_master.astype(jnp.bfloat16), "shard", axis=0, tiled=True)
+    params = jnp.concatenate(
+        lax.all_to_all(
+            jnp.stack([new_master.astype(jnp.bfloat16)] * lax.axis_size("shard")), "shard", 0, 0
+        ),
+        axis=0,
+    )
     return (new_master, new_moment_one, new_moment_two, direction, params)
 
 

time: 1020 us -> 956 us (0.937)
  the two profiles are of different devices: /device:TPU:8 before, /device:TPU:30 now
where the time goes in v1:
time: 956 us; the launch traced here: 955 us
  waiting for transfers between devices  829 us (87%)
  blocking collectives  104 us (11%)
  between operations  15.5 us (2%)
    unnamed x2, waiting for transfers between devices  829 us
    all_to_all x1, blocking collectives, local(): lax.all_to_all(jnp.stack([new_master.astype(jnp.bfloat16)] * lax.axis_siz...  79.5 us
    psum x1, blocking collectives, local(): summed = lax.psum(row_block, 'rep')  24.1 us
  transfers between devices with their start and end apart: 1, of which 1 were waited for; matrix products, arithmetic and copies ran while one was open for 0% of the time, Pallas kernels for 0%

profile of v1, /device:TPU:30, one launch (start us, length us, event | category | flops | bytes accessed | tf_op | source)
XLA Modules:
  0.0 955.5 jit_solution(9978984103658960192)
XLA Ops:
  7.2 0.0 all-reduce.3.cloned.1.call-start
  7.2 3.0 bitcast_convert_fusion
  10.2 0.0 copy-start
  10.2 0.0 copy-start.1
  10.2 0.0 copy-start.2
  10.2 0.0 all-reduce.3.cloned.1.call-update
  11.0 1.3 dynamic-slice
  13.0 828.8 %all-reduce.3.cloned.1.call-done = f32[576,1152]{1,0:T(8,128)} async-done(((f32[576,1152]{1,0:T(8,128)}), f32[576,1152]{1,0:T(8,128)}) %all-reduce.3.cloned.1.call-update) | async-done | bytes 2654224
  841.7 0.9 constant_dynamic-slice_fusion
  842.6 24.1 %psum.7 = f32[9,1152]{1,0:T(8,128)S(1)} all-reduce(f32[9,1152]{1,0:T(8,128)S(1)} %constant_dynamic-slice_fusion), channel_id=1, replica_groups=mesh['rep'=8,'shard'=64] {'rep'}, use_global_device_ids=true, to_apply=%region_1.0 | all-reduce | flops 10368 | bytes 82944 | tf_op jit(solution)/shard_map/psum | solution.py:27
  866.8 0.0 copy-done
  866.8 0.0 copy-done.1
  866.8 0.0 copy-done.2
  866.8 0.7 fusion
  867.6 0.2 stack.2
  867.7 79.5 %all_to_all.5 = bf16[64,9,1152]{2,1,0:T(8,128)(2,1)S(1)} all-to-all(bf16[64,9,1152]{2,1,0:T(8,128)(2,1)S(1)} %stack.2), channel_id=1, replica_groups=mesh['rep'=8,'shard'=64] {'shard'}, dimensions={0} | all-to-all | bytes 2654208 | tf_op jit(solution)/shard_map/all_to_all | solution.py:31
  947.2 1.4 reshape.27
Async XLA Ops:
  7.2 834.6 %all-reduce.3.cloned.1.call-start = ((), (), s32[]{:S(2)}) async-start(), calls=%async_computation.1 | async-start | bytes 5308416
  10.2 856.6 %copy-start = (f32[9,1152]{1,0:T(8,128)S(1)}, f32[9,1152]{1,0:T(8,128)}, u32[]{:S(2)}) copy-start(f32[9,1152]{1,0:T(8,128)} %param.6) | copy-start | bytes 124420
  10.2 856.6 %copy-start.1 = (f32[9,1152]{1,0:T(8,128)S(1)}, f32[9,1152]{1,0:T(8,128)}, u32[]{:S(2)}) copy-start(f32[9,1152]{1,0:T(8,128)} %param.8) | copy-start | bytes 124420
  10.2 856.6 %copy-start.2 = (f32[9,1152]{1,0:T(8,128)S(1)}, f32[9,1152]{1,0:T(8,128)}, u32[]{:S(2)}) copy-start(f32[9,1152]{1,0:T(8,128)} %param.7) | copy-start | bytes 124420
Sparse Core Ops, SparseCore 0:
  10.9 830.7 all-reduce.2
